TPU v7x, 32 devices: a whole 2x2x4 slice. The times are simulated.
32 devices in a mesh: tensor: 4 (over y, core), dp: 8 (over z, x).
Axes of the slice: x: 2, y: 2, z: 4, core: 2. Of those that a mesh axis runs over, the one named last changes fastest.
Arguments:
- hidden: bfloat16 [6144, 14336], P('dp', 'tensor'), may hold values from -6 to 6
- upstream: bfloat16 [6144, 4096], P('dp'), may hold values from -4 to 4
- head_weight: bfloat16 [14, 4096], replicated, may hold values from -2 to 2
- class_probs: float32 [6144, 14], P('dp'), as said below
- teacher_votes: int32 [6144, 14], P('dp'), may hold values from 0 to 7
- clean_flag: int32 [6144], P('dp'), may hold values from 0 to 1, as said below
Outputs:
- reweighted: bfloat16 [4096, 14336], P('dp', 'tensor')
Inputs may be any that keep to these rules, and one draw needn't show every extreme that they name: In each aligned block of 768 examples exactly 16 have clean_flag 1. `class_probs`: every row is positive and sums to one.
All inputs are finite; a program needn't handle non-finite values.
Results may differ from a plain program's by a relative error of at most 0.019.
Values may be sent and summed in bfloat16 or wider, within the bound.
A program may use at most 128 MiB of HBM per device.

v0:
```python
import jax
import jax.numpy as jnp
from jax import lax
from jax.sharding import PartitionSpec as P

D = 4096
F = 14336
CLEAN_DEV = 16


def gram(left, right):
    return lax.dot_general(
        left, right, (((1,), (1,)), ((), ())), preferred_element_type=jnp.float32
    )


def body(hidden, upstream, head_weight, class_probs, teacher_votes, clean_flag):
    examples = hidden.shape[0]
    classes = class_probs.shape[1]
    labels = jnp.argmax(teacher_votes, axis=1)
    onehot = (labels[:, None] == jnp.arange(classes, dtype=jnp.int32)[None, :]).astype(jnp.float32)
    errors = class_probs - onehot
    grad_out = (
        upstream.astype(jnp.float32)
        + jnp.dot(errors, head_weight.astype(jnp.float32), precision=lax.Precision.HIGHEST)
    ).astype(jnp.bfloat16)
    picked = jnp.argsort(1 - clean_flag, stable=True)[:CLEAN_DEV]
    clean_hidden = hidden[picked]
    all_hidden, all_grad = (
        lax.all_gather(clean_hidden, "dp", axis=0, tiled=True),
        lax.all_gather(grad_out[picked], "dp", axis=0, tiled=True),
    )
    local_scores = jnp.sum(gram(hidden, all_hidden) * gram(grad_out, all_grad), axis=1)
    scores = lax.psum(local_scores, "tensor")
    groups = lax.axis_size("dp")
    clean_total = groups * CLEAN_DEV
    noisy_total = groups * (examples - CLEAN_DEV)
    scores = scores / jnp.sqrt(jnp.float32(F) * jnp.float32(D) * jnp.float32(clean_total))
    weights = (
        jax.nn.softplus(scores)
        * (1 - clean_flag).astype(jnp.float32)
        / jnp.sqrt(jnp.float32(noisy_total))
    )
    weighted = (weights[:, None] * grad_out.astype(jnp.float32)).astype(jnp.bfloat16)
    return lax.psum_scatter(
        lax.dot_general(
            weighted, hidden, (((0,), (0,)), ((), ())), preferred_element_type=jnp.float32
        ).astype(jnp.bfloat16),
        "dp",
        scatter_dimension=0,
        tiled=True,
    )


def solution(mesh):
    return jax.shard_map(
        body,
        mesh=mesh,
        in_specs=(P("dp", "tensor"), P("dp", None), P(), P("dp", None), P("dp", None), P("dp")),
        out_specs=P("dp", "tensor"),
        check_vma=False,
    )
```

profile of v0, /device:TPU:0, one launch (start us, length us, event | category | flops | bytes accessed | tf_op | source)
XLA Modules:
  0.0 590.6 jit_solution(13295534719912838035)
XLA Ops:
  6.5 0.0 copy-start
  6.5 0.0 all-gather.4.cloned.1.call-start
  6.5 0.7 broadcast_subtract_fusion
  7.3 4.4 sort.17
  11.6 1.4 iota_reduce_fusion
  13.1 0.0 copy-done
  13.1 9.2 %add_convert_fusion = bf16[768,4096]{1,0:T(8,128)(2,1)} fusion(bf16[768,4096]{1,0:T(8,128)(2,1)} %param.7, bf16[14,4096]{1,0:T(8,128)(2,1)S(1)} %copy-done, f32[768,14]{0,1:T(8,128)} %param.9, s32[768]{0:T(1024)S(1)} %get-tuple-element.8), kind=kOutput, calls=%fused_computation.4 | convolution fusion | flops 537951744 | bytes 12743680 | tf_op jit(solution)/shard_map/dot_general | solution.py:25
  22.3 5.0 gather_fusion.1
  27.3 0.0 all-gather.4.cloned.1.call-update
  27.3 0.0 reduce-scatter.2.cloned.1.call-start
  27.4 4.0 gather_fusion
  31.4 35.9 %all-gather = bf16[128,3584]{1,0:T(8,128)(2,1)S(1)} all-gather(bf16[16,3584]{1,0:T(8,128)(2,1)S(1)} %gather_fusion), channel_id=2, replica_groups=mesh['tensor'=4,'dp'=8] {'dp'}, dimensions={0}, use_global_device_ids=true | all-gather | bytes 1032192 | tf_op jit(solution)/shard_map/all_gather | solution.py:30
  67.3 0.0 copy-start.1
  67.3 7.4 %all-gather.4.cloned.1.call-done = bf16[128,4096]{1,0:T(8,128)(2,1)} async-done(((bf16[16,4096]{1,0:T(8,128)(2,1)}), bf16[128,4096]{1,0:T(8,128)(2,1)}) %all-gather.4.cloned.1.call-update) | async-done | bytes 1048592 | tf_op jit(solution)/shard_map/all_gather | solution.py:31
  74.7 5.2 fusion.8
  80.0 4.4 fusion.2
  84.4 6.0 %psum.7 = f32[768]{0:T(1024)S(1)} all-reduce(f32[768]{0:T(1024)S(1)} %fusion.2), channel_id=1, replica_groups=mesh['tensor'=4,'dp'=8] {'tensor'}, use_global_device_ids=true, to_apply=%region_3.4 | all-reduce | flops 768 | bytes 6144 | tf_op jit(solution)/shard_map/psum | solution.py:34
  90.4 0.0 copy-done.1
  90.4 30.3 %convolution_convert_fusion = bf16[4096,3584]{1,0:T(8,128)(2,1)} fusion(bf16[768,3584]{1,0:T(8,128)(2,1)} %param.6, bf16[768,4096]{1,0:T(8,128)(2,1)} %add_convert_fusion, f32[768]{0:T(1024)S(1)} %fusion.7), kind=kOutput, calls=%fused_computation.2 | convolution fusion | flops 22572695552 | bytes 41159680 | tf_op jit(solution)/shard_map/dot_general | solution.py:46
  120.7 0.0 reduce-scatter.2.cloned.1.call-update
  120.7 463.0 %reduce-scatter.2.cloned.1.call-done = bf16[512,3584]{1,0:T(8,128)(2,1)} async-done(((bf16[4096,3584]{1,0:T(8,128)(2,1)}), bf16[512,3584]{1,0:T(8,128)(2,1)}) %reduce-scatter.2.cloned.1.call-update) | async-done | bytes 3670032 | tf_op jit(solution)/shard_map/reduce_scatter | solution.py:45
  (4 shorter events, 0.0 us)
Async XLA Ops:
  6.5 6.5 %copy-start = (bf16[14,4096]{1,0:T(8,128)(2,1)S(1)}, bf16[14,4096]{1,0:T(8,128)(2,1)}, u32[]{:S(2)}) copy-start(bf16[14,4096]{1,0:T(8,128)(2,1)} %param.8) | copy-start | bytes 344068
  6.5 68.2 %all-gather.4.cloned.1.call-start = ((), (), s32[]{:S(2)}) async-start(), calls=%async_computation.2 | async-start | bytes 1179648 | tf_op jit(solution)/shard_map/all_gather | solution.py:31
  27.3 556.5 %reduce-scatter.2.cloned.1.call-start = ((), (), s32[]{:S(2)}) async-start(), calls=%async_computation.1 | async-start | bytes 33030144 | tf_op jit(solution)/shard_map/reduce_scatter | solution.py:45
  67.3 23.1 %copy-start.1 = (s32[768]{0:T(1024)S(1)}, s32[768]{0:T(1024)}, u32[]{:S(2)}) copy-start(s32[768]{0:T(1024)} %param.11) | copy-start | bytes 9220
Sparse Core Ops, SparseCore 0:
  27.4 47.2 all-gather.3
  120.8 462.8 reduce-scatter.1
where the time goes:
time: 591 us
  waiting for transfers between devices  471 us (80%)
  matrix products  49.2 us (8%)
  blocking collectives  41.9 us (7%)
  between operations  13.4 us (2%)
  local copies, waits for them, and re-layouts  9 us (2%)
  other arithmetic  6.54 us (1%)
    reduce_scatter x1, waiting for transfers between devices, body(): lax.psum_scatter(lax.dot_general(weighted, hidden, (((0,), (0,)), ((), ()...  463 us
    all_gather x1, blocking collectives, body(): lax.all_gather(clean_hidden, 'dp', axis=0, tiled=True)  35.9 us
    dot_general x1, matrix products, body(): lax.dot_general(weighted, hidden, (((0,), (0,)), ((), ())), preferred_ele...  30.3 us
  transfers between devices with their start and end apart: 2, of which 2 were waited for; matrix products, arithmetic and copies ran while one was open for 1% of the time, Pallas kernels for 0%

commit v1 on v0

v1 whole, which is shorter than its diff:
```python
import jax
import jax.numpy as jnp
from jax import lax
from jax.sharding import PartitionSpec as P

CLEAN_DEV = 16
CHUNKS = 4


def gram(left, right):
    return lax.dot_general(
        left, right, (((1,), (1,)), ((), ())), preferred_element_type=jnp.float32
    )


def gradient(upstream, errors, head_weight):
    first = lax.reduce_precision(errors, 8, 7)
    second = lax.reduce_precision(errors - first, 8, 7)
    third = errors - first - second
    terms = jnp.concatenate([first, second, third], axis=1).astype(jnp.bfloat16)
    heads = jnp.concatenate([head_weight] * 3, axis=0)
    product = jnp.dot(terms, heads, preferred_element_type=jnp.float32)
    return (upstream.astype(jnp.float32) + product).astype(jnp.bfloat16)


def exchange(array, bit):
    size = lax.axis_size("dp")
    return lax.ppermute(array, "dp", [(i, i ^ bit) for i in range(size)])


def body(hidden, upstream, head_weight, class_probs, teacher_votes, clean_flag):
    examples, units = hidden.shape
    width = upstream.shape[1]
    classes = class_probs.shape[1]
    groups = lax.axis_size("dp")
    me = lax.axis_index("dp")
    high = groups // 4
    rows = width // groups
    part = rows // CHUNKS
    low_bit, mid_bit, high_index = me % 2, (me // 2) % 2, me // 4

    partner_hidden = exchange(hidden, 2)

    labels = jnp.argmax(teacher_votes, axis=1)
    onehot = (labels[:, None] == jnp.arange(classes, dtype=jnp.int32)[None, :]).astype(jnp.float32)
    grad_out = gradient(upstream, class_probs - onehot, head_weight)

    place = jnp.arange(examples, dtype=jnp.int32)
    order = jnp.sum(jnp.where(place[None, :] <= place[:, None], clean_flag[None, :], 0), axis=1)
    slots = jnp.arange(1, CLEAN_DEV + 1, dtype=jnp.int32)
    pick = ((order[None, :] == slots[:, None]) & (clean_flag[None, :] == 1)).astype(jnp.bfloat16)
    clean_hidden = jnp.dot(pick, hidden, preferred_element_type=jnp.float32).astype(jnp.bfloat16)
    clean_grad = jnp.dot(pick, grad_out, preferred_element_type=jnp.float32).astype(jnp.bfloat16)
    all_hidden = lax.all_gather(clean_hidden, "dp", axis=0, tiled=True)
    all_grad = lax.all_gather(clean_grad, "dp", axis=0, tiled=True)

    split = grad_out.reshape(examples, high, 2, 2 * rows)
    own_half = lax.dynamic_index_in_dim(split, mid_bit, 2, keepdims=False)
    other_half = lax.dynamic_index_in_dim(split, 1 - mid_bit, 2, keepdims=False)
    other_half = other_half.reshape(examples, width // 2)
    partner_grad = exchange(other_half, 2)
    own_grad = own_half.reshape(examples, width // 2)

    local_scores = jnp.sum(gram(hidden, all_hidden) * gram(grad_out, all_grad), axis=1)
    scores = lax.psum(local_scores, "tensor")
    clean_total = groups * CLEAN_DEV
    noisy_total = groups * (examples - CLEAN_DEV)
    units_total = units * lax.axis_size("tensor")
    scores = scores / jnp.sqrt(jnp.float32(units_total) * jnp.float32(width) * jnp.float32(clean_total))
    weights = (
        jax.nn.softplus(scores)
        * (1 - clean_flag).astype(jnp.float32)
        / jnp.sqrt(jnp.float32(noisy_total))
    )
    both_weights = jnp.concatenate([weights, exchange(weights, 2)])
    both_hidden = jnp.concatenate([hidden, partner_hidden], axis=0)
    both_grad = jnp.concatenate([own_grad, partner_grad], axis=0)
    weighted = (both_weights[:, None] * both_grad.astype(jnp.float32)).astype(jnp.bfloat16)
    weighted = weighted.reshape(2 * examples, high, 2, CHUNKS, part)
    keep_all = lax.dynamic_index_in_dim(weighted, low_bit, 2, keepdims=False)
    send_all = lax.dynamic_index_in_dim(weighted, 1 - low_bit, 2, keepdims=False)

    def product(block):
        return lax.dot_general(
            block.reshape(2 * examples, high * part), both_hidden, (((0,), (0,)), ((), ())),
            preferred_element_type=jnp.float32,
        )

    pieces = []
    for chunk in range(CHUNKS):
        sent = product(send_all[:, :, chunk]).astype(jnp.bfloat16)
        arrived = exchange(sent, 1)
        total = (product(keep_all[:, :, chunk]) + arrived.astype(jnp.float32)).astype(jnp.bfloat16)
        size, bit = high, 4 * (high // 2)
        while size > 1:
            total = total.reshape(2, size // 2 * part, units)
            upper = (high_index // (size // 2)) % 2
            keep = lax.dynamic_index_in_dim(total, upper, 0, keepdims=False)
            give = lax.dynamic_index_in_dim(total, 1 - upper, 0, keepdims=False)
            arrived = exchange(give, bit)
            total = (keep.astype(jnp.float32) + arrived.astype(jnp.float32)).astype(jnp.bfloat16)
            size, bit = size // 2, bit // 2
        pieces.append(total)
    return jnp.concatenate(pieces, axis=0)


def solution(mesh):
    return jax.shard_map(
        body,
        mesh=mesh,
        in_specs=(P("dp", "tensor"), P("dp", None), P(), P("dp", None), P("dp", None), P("dp")),
        out_specs=P("dp", "tensor"),
        check_vma=False,
    )
```

time: 591 us -> 532 us (0.900)
  waiting for transfers between devices: 471 us -> 177 us
  blocking collectives: 41.9 us -> 176 us
  local copies, waits for them, and re-layouts: 9 us -> 94.5 us
  starting transfers between devices: 0.04 us -> 11.9 us
    reduce_scatter x1 -> x0, waiting for transfers between devices: 463 us -> none  [body(): lax.psum_scatter(lax.dot_general(weighted, hidden, (((0,), (0,)), ((), ()...]
    ppermute x0 -> x11, waiting for transfers between devices: none -> 177 us  [exchange(): return lax.ppermute(array, 'dp', [(i, i ^ bit) for i in range(size)])]
    all_gather x1, blocking collectives: 35.9 us -> 170 us  [body(): all_hidden = lax.all_gather(clean_hidden, 'dp', axis=0, tiled=True)]
    unnamed x4 -> x31, local copies, waits for them, and re-layouts: 0.01 us -> 36.5 us
    dynamic_slice x0 -> x4, local copies, waits for them, and re-layouts: none -> 26.2 us  [the longest x1 15.9 us: body(): own_half = lax.dynamic_index_in_dim(split, mid_bit, 2, keepdims=False)]
    slice x0 -> x10, local copies, waits for them, and re-layouts: none -> 14.9 us  [the longest x5 8.82 us: body(): sent = product(send_all[:, :, chunk]).astype(jnp.bfloat16)]
    ppermute x0 -> x11, starting transfers between devices: none -> 11.9 us  [exchange(): return lax.ppermute(array, 'dp', [(i, i ^ bit) for i in range(size)])]
    reshape x0 -> x1, local copies, waits for them, and re-layouts: none -> 11.1 us  [body(): split = grad_out.reshape(examples, high, 2, 2 * rows)]
  transfers between devices with their start and end apart: 2 -> 12, of which waited for: 2 -> 6; matrix products, arithmetic and copies ran while one was open for 1% -> 25% of each run, Pallas kernels for 0% -> 0%
where the time goes in v1:
time: 532 us; the launch traced here: 530 us
  waiting for transfers between devices  177 us (33%)
  blocking collectives  176 us (33%)
  local copies, waits for them, and re-layouts  94.5 us (18%)
  matrix products  48.3 us (9%)
  between operations  13.8 us (3%)
  starting transfers between devices  11.9 us (2%)
  other arithmetic  9.02 us (2%)
    ppermute x11, waiting for transfers between devices, exchange(): return lax.ppermute(array, 'dp', [(i, i ^ bit) for i in range(size)])  177 us
    all_gather x1, blocking collectives, body(): all_hidden = lax.all_gather(clean_hidden, 'dp', axis=0, tiled=True)  170 us
    unnamed x31, local copies, waits for them, and re-layouts  36.5 us
    dot_general x8, matrix products, product(): lax.dot_general(block.reshape(2 * examples, high * part), both_hidden, ((...  28.7 us
    dynamic_slice x1, local copies, waits for them, and re-layouts, body(): own_half = lax.dynamic_index_in_dim(split, mid_bit, 2, keepdims=False)  15.9 us
    ppermute x11, starting transfers between devices, exchange(): return lax.ppermute(array, 'dp', [(i, i ^ bit) for i in range(size)])  11.9 us
    reshape x1, local copies, waits for them, and re-layouts, body(): split = grad_out.reshape(examples, high, 2, 2 * rows)  11.1 us
  transfers between devices with their start and end apart: 12, of which 6 were waited for; matrix products, arithmetic and copies ran while one was open for 25% of the time, Pallas kernels for 0%

profile of v1, /device:TPU:0, one launch (start us, length us, event | category | flops | bytes accessed | tf_op | source)
XLA Modules:
  0.0 530.3 jit_solution(115440441244654834)
XLA Ops:
  12.6 4.8 add_convert_fusion
  21.8 11.1 %reshape.48 = bf16[768,2,2,1024]{3,2,1,0:T(2,128)(2,1)} reshape(bf16[768,4096]{1,0:T(8,128)(2,1)} %copy-done.2) | data formatting | bytes 12582912 | tf_op jit(solution)/shard_map/reshape | solution.py:57
  32.9 15.9 %constant_dynamic-slice_fusion.3 = (bf16[768,2,1,1024]{3,2,1,0:T(2,128)(2,1)}, bf16[768,2,1,1024]{3,2,1,0:T(2,128)(2,1)}) fusion(bf16[768,2,2,1024]{3,2,1,0:T(2,128)(2,1)} %reshape.48, s32[]{:T(128)S(6)} %select_n.75, s32[]{:T(128)S(6)} %select_n.76), kind=kLoop, calls=%fused_computation.68 | loop fusion | bytes 12582920 | tf_op jit(solution)/shard_map/jit(dynamic_index_in_dim)/dynamic_slice | solution.py:58
  48.8 15.1 %copy.34 = bf16[768,2,1,1024]{0,3,1,2:T(8,128)(2,1)} copy(bf16[768,2,1,1024]{3,2,1,0:T(2,128)(2,1)} %get-tuple-element.10) | data formatting | bytes 6291456
  64.0 3.4 convolution_convert_fusion.5
  67.4 170.3 %all_gather.6 = bf16[128,3584]{1,0:T(8,128)(2,1)S(1)} all-gather(bf16[16,3584]{1,0:T(8,128)(2,1)S(1)} %convolution_convert_fusion.5), channel_id=1, replica_groups=mesh['tensor'=4,'dp'=8] {'dp'}, dimensions={0}, use_global_device_ids=true | all-gather | bytes 1032192 | tf_op jit(solution)/shard_map/all_gather | solution.py:54
  237.8 5.2 fusion.32
  243.0 4.4 fusion.9
  247.4 5.7 %psum.7 = f32[768]{0:T(1024)S(1)} all-reduce(f32[768]{0:T(1024)S(1)} %fusion.9), channel_id=1, replica_groups=mesh['tensor'=4,'dp'=8] {'tensor'}, use_global_device_ids=true, to_apply=%region_3.4 | all-reduce | flops 768 | bytes 6144 | tf_op jit(solution)/shard_map/psum | solution.py:65
  253.2 5.3 %constant_dynamic-update-slice_fusion.1 = bf16[1536,3584]{1,0:T(8,128)(2,1)} fusion(bf16[768,3584]{1,0:T(8,128)(2,1)} %param.6), kind=kLoop, calls=%fused_computation.62 | loop fusion | bytes 11010048
  258.5 13.3 %copy.33 = bf16[768,2,1,1024]{0,3,1,2:T(8,128)(2,1)S(1)} copy(bf16[768,2,1,1024]{3,2,1,0:T(2,128)(2,1)} %get-tuple-element.9) | data formatting | bytes 6291456
  271.9 3.2 multiply_convert_fusion
  275.1 3.3 constant_dynamic-slice_fusion
  278.4 3.5 copy.25
  290.8 3.5 copy.23
  300.4 5.4 %constant_dynamic-update-slice_fusion = bf16[1536,3584]{1,0:T(8,128)(2,1)} fusion(bf16[1536,3584]{1,0:T(8,128)(2,1)} %constant_dynamic-update-slice_fusion.1, bf16[768,3584]{1,0:T(8,128)(2,1)} %collective-permute-done.2), kind=kLoop, calls=%fused_computation.61 | loop fusion | bytes 11010048 | tf_op jit(solution)/shard_map/concatenate | solution.py:76
  305.8 7.3 %convolution_convert_fusion.2 = bf16[256,3584]{1,0:T(8,128)(2,1)S(1)} fusion(bf16[1536,256]{0,1:T(8,128)(2,1)S(1)} %bitcast.83, bf16[1536,3584]{1,0:T(8,128)(2,1)} %constant_dynamic-update-slice_fusion), kind=kOutput, calls=%fused_computation.12 | convolution fusion | flops 2819489792 | bytes 13631488 | tf_op jit(solution)/shard_map/dot_general | solution.py:84
  326.5 32.7 %collective-permute-done.3 = bf16[256,3584]{1,0:T(8,128)(2,1)S(1)} collective-permute-done((bf16[256,3584]{1,0:T(8,128)(2,1)S(1)}, bf16[256,3584]{1,0:T(8,128)(2,1)S(1)}, u32[]{:S(2)}, u32[]{:S(2)}) %collective-permute-start.3) | collective-permute-done | bytes 1835040 | tf_op jit(solution)/shard_map/ppermute | solution.py:28
  363.5 35.0 %collective-permute-done.5 = bf16[256,3584]{1,0:T(8,128)(2,1)S(1)} collective-permute-done((bf16[256,3584]{1,0:T(8,128)(2,1)S(1)}, bf16[256,3584]{1,0:T(8,128)(2,1)S(1)}, u32[]{:S(2)}, u32[]{:S(2)}) %collective-permute-start.5) | collective-permute-done | bytes 1835040 | tf_op jit(solution)/shard_map/ppermute | solution.py:28
  398.5 3.3 fusion.1
  403.1 34.7 %collective-permute-done.7 = bf16[256,3584]{1,0:T(8,128)(2,1)S(1)} collective-permute-done((bf16[256,3584]{1,0:T(8,128)(2,1)S(1)}, bf16[256,3584]{1,0:T(8,128)(2,1)S(1)}, u32[]{:S(2)}, u32[]{:S(2)}) %collective-permute-start.7) | collective-permute-done | bytes 1835040 | tf_op jit(solution)/shard_map/ppermute | solution.py:28
  437.8 3.1 fusion.2
  442.2 33.9 %collective-permute-done.9 = bf16[256,3584]{1,0:T(8,128)(2,1)S(1)} collective-permute-done((bf16[256,3584]{1,0:T(8,128)(2,1)S(1)}, bf16[256,3584]{1,0:T(8,128)(2,1)S(1)}, u32[]{:S(2)}, u32[]{:S(2)}) %collective-permute-start.9) | collective-permute-done | bytes 1835040 | tf_op jit(solution)/shard_map/ppermute | solution.py:28
  482.4 38.9 %collective-permute-done.10 = bf16[128,3584]{1,0:T(8,128)(2,1)S(1)} collective-permute-done((bf16[128,3584]{1,0:T(8,128)(2,1)S(1)}, bf16[128,3584]{1,0:T(8,128)(2,1)S(1)}, u32[]{:S(2)}, u32[]{:S(2)}) %collective-permute-start.10) | collective-permute-done | bytes 917536 | tf_op jit(solution)/shard_map/ppermute | solution.py:28
  (80 shorter events, 53.9 us)
Async XLA Ops:
  6.5 4.6 copy-start
  6.5 231.2 %all-gather.2.cloned.1.call-start = ((), (), s32[]{:S(2)}) async-start(), calls=%async_computation | async-start | bytes 1179648 | tf_op jit(solution)/shard_map/all_gather | solution.py:55
  6.5 293.8 %collective-permute-start.2 = (bf16[768,3584]{1,0:T(8,128)(2,1)}, bf16[768,3584]{1,0:T(8,128)(2,1)}, u32[]{:S(2)}, u32[]{:S(2)}) collective-permute-start(bf16[768,3584]{1,0:T(8,128)(2,1)} %param.6), channel_id=1, source_target_pairs={{0,2},{1,3},{2,0},{3,1},{4,6},{5,7},{6,4},{7,5},{8,10},{9,11},{10,... | collective-permute-start | bytes 16515080 | tf_op jit(solution)/shard_map/ppermute | solution.py:28
  63.9 208.0 %collective-permute-start.1 = (bf16[768,2048]{0,1:T(8,128)(2,1)}, bf16[768,2048]{0,1:T(8,128)(2,1)}, u32[]{:S(2)}, u32[]{:S(2)}) collective-permute-start(bf16[768,2048]{0,1:T(8,128)(2,1)} %bitcast.2), channel_id=1, source_target_pairs={{0,2},{1,3},{2,0},{3,1},{4,6},{5,7},{6,4},{7,5},{8,10},{9,11},{10,... | collective-permute-start | bytes 9437192 | tf_op jit(solution)/shard_map/ppermute | solution.py:28
  243.0 10.1 %copy-start.13 = (s32[768]{0:T(1024)S(1)}, s32[768]{0:T(1024)}, u32[]{:S(2)}) copy-start(s32[768]{0:T(1024)} %param.11) | copy-start | bytes 9220
  253.1 18.7 %collective-permute-start = (f32[768]{0:T(1024)S(1)}, f32[768]{0:T(1024)S(1)}, u32[]{:S(2)}, u32[]{:S(2)}) collective-permute-start(f32[768]{0:T(1024)S(1)} %fusion.28), channel_id=1, source_target_pairs={{0,2},{1,3},{2,0},{3,1},{4,6},{5,7},{6,4},{7,5},{8,10},{9,11},{10,... | collective-permute-start | bytes 9224 | tf_op jit(solution)/shard_map/ppermute | solution.py:28
  283.6 4.7 copy-start.5
  283.6 5.9 %copy-start.3 = (bf16[1536,2,1,128]{3,0,2,1:T(8,128)(2,1)S(1)}, bf16[1536,2,1,128]{3,0,2,1:T(8,128)(2,1)}, u32[]{:S(2)}) copy-start(bf16[1536,2,1,128]{3,0,2,1:T(8,128)(2,1)} %get-tuple-element.14) | copy-start | bytes 2359300
  296.0 3.8 copy-start.6
  296.0 4.1 copy-start.4
  300.4 5.5 %copy-start.12 = (bf16[1536,2,1,128]{0,3,1,2:T(8,128)(2,1)S(1)}, bf16[1536,2,1,128]{0,3,1,2:T(8,128)(2,1)}, u32[]{:S(2)}) copy-start(bf16[1536,2,1,128]{0,3,1,2:T(8,128)(2,1)} %copy.28) | copy-start | bytes 2359300
  305.8 7.3 %copy-start.7 = (bf16[1536,3584]{1,0:T(8,128)(2,1)S(1)}, bf16[1536,3584]{1,0:T(8,128)(2,1)}, u32[]{:S(2)}) copy-start(bf16[1536,3584]{1,0:T(8,128)(2,1)} %constant_dynamic-update-slice_fusion) | copy-start | bytes 33030148
  305.8 7.4 %copy-start.11 = (bf16[1536,2,1,128]{0,3,1,2:T(8,128)(2,1)S(1)}, bf16[1536,2,1,128]{0,3,1,2:T(8,128)(2,1)}, u32[]{:S(2)}) copy-start(bf16[1536,2,1,128]{0,3,1,2:T(8,128)(2,1)} %copy.26) | copy-start | bytes 2359300
  313.2 5.1 copy-start.8
  316.2 43.0 %collective-permute-start.3 = (bf16[256,3584]{1,0:T(8,128)(2,1)S(1)}, bf16[256,3584]{1,0:T(8,128)(2,1)S(1)}, u32[]{:S(2)}, u32[]{:S(2)}) collective-permute-start(bf16[256,3584]{1,0:T(8,128)(2,1)S(1)} %convolution_convert_fusion.3), channel_id=1, source_target_pairs={{0,1},{1,0},{2,3},{3,2},{4,5},{5,4},{6,7},{7,6},{8,9},{9,8},{10,11... | collective-permute-start | bytes 5505032 | tf_op jit(solution)/shard_map/ppermute | solution.py:28
  316.3 82.2 %collective-permute-start.5 = (bf16[256,3584]{1,0:T(8,128)(2,1)S(1)}, bf16[256,3584]{1,0:T(8,128)(2,1)S(1)}, u32[]{:S(2)}, u32[]{:S(2)}) collective-permute-start(bf16[256,3584]{1,0:T(8,128)(2,1)S(1)} %convolution_convert_fusion.2), channel_id=1, source_target_pairs={{0,1},{1,0},{2,3},{3,2},{4,5},{5,4},{6,7},{7,6},{8,9},{9,8},{10,11... | collective-permute-start | bytes 5505032 | tf_op jit(solution)/shard_map/ppermute | solution.py:28
  318.3 3.0 copy-start.9
  321.4 37.8 %copy-start.10 = (bf16[1536,2,1,128]{0,3,1,2:T(8,128)(2,1)S(1)}, bf16[1536,2,1,128]{0,3,1,2:T(8,128)(2,1)}, u32[]{:S(2)}) copy-start(bf16[1536,2,1,128]{0,3,1,2:T(8,128)(2,1)} %copy.24) | copy-start | bytes 2359300
  324.4 113.5 %collective-permute-start.7 = (bf16[256,3584]{1,0:T(8,128)(2,1)S(1)}, bf16[256,3584]{1,0:T(8,128)(2,1)S(1)}, u32[]{:S(2)}, u32[]{:S(2)}) collective-permute-start(bf16[256,3584]{1,0:T(8,128)(2,1)S(1)} %convolution_convert_fusion.1), channel_id=1, source_target_pairs={{0,1},{1,0},{2,3},{3,2},{4,5},{5,4},{6,7},{7,6},{8,9},{9,8},{10,11... | collective-permute-start | bytes 5505032 | tf_op jit(solution)/shard_map/ppermute | solution.py:28
  324.5 151.5 %collective-permute-start.9 = (bf16[256,3584]{1,0:T(8,128)(2,1)S(1)}, bf16[256,3584]{1,0:T(8,128)(2,1)S(1)}, u32[]{:S(2)}, u32[]{:S(2)}) collective-permute-start(bf16[256,3584]{1,0:T(8,128)(2,1)S(1)} %convolution_convert_fusion), channel_id=1, source_target_pairs={{0,1},{1,0},{2,3},{3,2},{4,5},{5,4},{6,7},{7,6},{8,9},{9,8},{10,11... | collective-permute-start | bytes 5505032 | tf_op jit(solution)/shard_map/ppermute | solution.py:28
  362.3 117.8 %collective-permute-start.4 = (bf16[128,3584]{1,0:T(8,128)(2,1)S(1)}, bf16[128,3584]{1,0:T(8,128)(2,1)S(1)}, u32[]{:S(2)}, u32[]{:S(2)}) collective-permute-start(bf16[128,3584]{1,0:T(8,128)(2,1)S(1)} %dynamic-slice_bitcast_fusion.3), channel_id=1, source_target_pairs={{0,4},{1,5},{2,6},{3,7},{4,0},{5,1},{6,2},{7,3},{8,12},{9,13},{10,... | collective-permute-start | bytes 2752520 | tf_op jit(solution)/shard_map/ppermute | solution.py:28
  401.9 78.4 %collective-permute-start.6 = (bf16[128,3584]{1,0:T(8,128)(2,1)S(1)}, bf16[128,3584]{1,0:T(8,128)(2,1)S(1)}, u32[]{:S(2)}, u32[]{:S(2)}) collective-permute-start(bf16[128,3584]{1,0:T(8,128)(2,1)S(1)} %dynamic-slice_bitcast_fusion.2), channel_id=1, source_target_pairs={{0,4},{1,5},{2,6},{3,7},{4,0},{5,1},{6,2},{7,3},{8,12},{9,13},{10,... | collective-permute-start | bytes 2752520 | tf_op jit(solution)/shard_map/ppermute | solution.py:28
  441.0 41.2 %collective-permute-start.8 = (bf16[128,3584]{1,0:T(8,128)(2,1)S(1)}, bf16[128,3584]{1,0:T(8,128)(2,1)S(1)}, u32[]{:S(2)}, u32[]{:S(2)}) collective-permute-start(bf16[128,3584]{1,0:T(8,128)(2,1)S(1)} %dynamic-slice_bitcast_fusion.1), channel_id=1, source_target_pairs={{0,4},{1,5},{2,6},{3,7},{4,0},{5,1},{6,2},{7,3},{8,12},{9,13},{10,... | collective-permute-start | bytes 2752520 | tf_op jit(solution)/shard_map/ppermute | solution.py:28
  479.2 42.1 %collective-permute-start.10 = (bf16[128,3584]{1,0:T(8,128)(2,1)S(1)}, bf16[128,3584]{1,0:T(8,128)(2,1)S(1)}, u32[]{:S(2)}, u32[]{:S(2)}) collective-permute-start(bf16[128,3584]{1,0:T(8,128)(2,1)S(1)} %dynamic-slice_bitcast_fusion), channel_id=1, source_target_pairs={{0,4},{1,5},{2,6},{3,7},{4,0},{5,1},{6,2},{7,3},{8,12},{9,13},{10,... | collective-permute-start | bytes 2752520 | tf_op jit(solution)/shard_map/ppermute | solution.py:28
  (2 other events, 4.8 us)
Sparse Core Ops, SparseCore 0:
  21.8 45.1 all-gather.1
